TPU v7x, 32 devices: a whole 2x2x4 slice. The times are simulated.
32 devices in a mesh: section: 4 (over y, x), expert: 8 (over z, core).
Axes of the slice: x: 2, y: 2, z: 4, core: 2. Of those that a mesh axis runs over, the one named last changes fastest.
Arguments:
- tokens: bfloat16 [6, 192, 1440], P(None, 'expert'), may hold values from -36 to 36
- norm_gain: float32 [4, 1440], P('section'), may hold values from 0.5 to 1.5
- gate_up: bfloat16 [4, 8, 1440, 2880], P('section', 'expert'), may hold values from -0.15625 to 0.15625
- down: bfloat16 [4, 8, 1440, 1440], P('section', 'expert'), may hold values from -0.15625 to 0.15625
- routes: int32 [4, 6, 192, 4], P('section', None, 'expert'), may hold values from 0 to 7, all different within a row; in each aligned block of 24 rows (0 to 23, 24 to 47, ..., all dimensions but the last counted through in order) at most 18 rows name the same one
- route_weights: int32 [4, 6, 192, 4], P('section', None, 'expert'), may hold values from 1 to 4095
Outputs:
- layer_outputs: bfloat16 [4, 6, 192, 1440], P('section', None, 'expert')
Inputs may be any that keep to these rules, and one draw needn't show every extreme that they name: `routes`: each token names 4 different experts; among the 24 tokens of one index of expert in one micro-batch of one layer, no expert is named by more than 18 tokens, a bound that some block reaches.
All inputs are finite; a program needn't handle non-finite values.
Results may differ from a plain program's by a relative error of at most 0.007.
Values may be sent and summed in bfloat16 or wider, within the bound.
A program may use at most 64 MiB of HBM per device.

v0:
```python
import jax
import jax.numpy as jnp
from jax import lax
from jax.sharding import PartitionSpec as P


def passed_along(value, axis, steps):
    count = lax.axis_size(axis)
    leading, last = (max(0, -steps), min(count, count - steps))
    return lax.ppermute(value, axis, [(source, source + steps) for source in range(leading, last)])


def expert_ffn(arrived, gate_up_w, down_w):
    senders, slot_count, width = arrived.shape
    hidden_units = down_w.shape[0]
    flat_rows = arrived.reshape(senders * slot_count, width)
    projected = jnp.dot(flat_rows, gate_up_w, preferred_element_type=jnp.float32)
    gate_part = projected[:, :hidden_units]
    up_part = projected[:, hidden_units:]
    activated = (gate_part * jax.nn.sigmoid(1.702 * gate_part) * (up_part + 1.0)).astype(
        jnp.bfloat16
    )
    result_rows = jnp.dot(activated, down_w, preferred_element_type=jnp.float32).astype(
        jnp.bfloat16
    )
    return result_rows.reshape(senders, slot_count, width)


def layer_step(stream, gain_row, gate_up_w, down_w, route_rows, weight_rows):
    token_count, chosen = route_rows.shape
    width = stream.shape[1]
    experts_n = lax.axis_size("expert")
    capacity = max(2, token_count * chosen * 3 // (2 * experts_n))
    widened = stream.astype(jnp.float32)
    scale = lax.rsqrt(jnp.mean(widened * widened, axis=-1, keepdims=True) + 1e-05)
    normed = (widened * scale * gain_row[None, :]).astype(jnp.bfloat16)
    flat_routes = route_rows.reshape(-1)
    matches = (flat_routes[:, None] == jnp.arange(experts_n, dtype=jnp.int32)[None, :]).astype(
        jnp.int32
    )
    slot_index = jnp.sum((jnp.cumsum(matches, axis=0) - 1) * matches, axis=1)
    target = flat_routes * capacity + slot_index
    placing = (
        jnp.arange(experts_n * capacity, dtype=jnp.int32)[:, None] == target[None, :]
    ).astype(jnp.bfloat16)
    repeated = jnp.repeat(normed, chosen, axis=0)
    outgoing = jnp.dot(placing, repeated, preferred_element_type=jnp.float32).astype(jnp.bfloat16)
    outgoing = outgoing.reshape(experts_n, capacity, width)
    arrived = lax.all_to_all(outgoing, "expert", split_axis=0, concat_axis=0, tiled=True)
    computed = expert_ffn(arrived, gate_up_w, down_w)
    returned = lax.all_to_all(computed, "expert", split_axis=0, concat_axis=0, tiled=True)
    returned_rows = returned.reshape(experts_n * capacity, width)
    gathered = jnp.take(returned_rows, target, axis=0).reshape(token_count, chosen, width)
    fixed_point = weight_rows.astype(jnp.float32)
    shares = fixed_point / jnp.sum(fixed_point, axis=-1, keepdims=True)
    accumulated = widened
    for branch in range(chosen):
        accumulated = accumulated + shares[:, branch : branch + 1] * gathered[:, branch].astype(
            jnp.float32
        )
    return accumulated.astype(jnp.bfloat16)


def shards(tokens, norm_gain, gate_up, down, routes, route_weights):
    micro_count, token_count, width = tokens.shape
    sections = lax.axis_size("section")
    section_index = lax.axis_index("section")
    gain_row = norm_gain[0]
    gate_up_w = gate_up[0, 0]
    down_w = down[0, 0]
    incoming = jnp.zeros((token_count, width), jnp.bfloat16)
    results = jnp.zeros((micro_count, token_count, width), jnp.bfloat16)
    tick_total = micro_count + sections - 1
    for tick_number in range(tick_total):
        fresh_input = tokens[min(tick_number, micro_count - 1)]
        stream = jnp.where(section_index == 0, fresh_input, incoming)
        micro_here = tick_number - section_index
        clamped = jnp.clip(micro_here, 0, micro_count - 1)
        route_rows = lax.dynamic_index_in_dim(routes[0], clamped, 0, keepdims=False)
        weight_rows = lax.dynamic_index_in_dim(route_weights[0], clamped, 0, keepdims=False)
        output_rows = layer_step(stream, gain_row, gate_up_w, down_w, route_rows, weight_rows)
        active = jnp.logical_and(micro_here >= 0, micro_here < micro_count)
        updated = lax.dynamic_update_index_in_dim(results, output_rows, clamped, 0)
        results = jnp.where(active, updated, results)
        if tick_number + 1 < tick_total:
            incoming = passed_along(output_rows, "section", 1)
    return results[None]


def solution(mesh):
    return jax.shard_map(
        shards,
        mesh=mesh,
        in_specs=(
            P(None, "expert", None),
            P("section", None),
            P("section", "expert", None, None),
            P("section", "expert", None, None),
            P("section", None, "expert", None),
            P("section", None, "expert", None),
        ),
        out_specs=P("section", None, "expert", None),
        check_vma=False,
    )
```

profile of v0, /device:TPU:4, one launch (start us, length us, event | category | flops | bytes accessed | tf_op | source)
XLA Modules:
  0.0 537.4 jit_solution(12916322955817120074)
XLA Ops:
  5.6 4.9 all-to-all-start
  11.0 16.2 %all-to-all-done = bf16[8,18,1440]{2,1,0:T(8,128)(2,1)S(1)} async-done(((bf16[8,18,1440]{2,1,0:T(8,128)(2,1)}), bf16[8,18,1440]{2,1,0:T(8,128)(2,1)S(1)}, u32[]{:S(2)}, u32[]{:S(2)}) %all-to-all-start) | async-done | bytes 414752 | tf_op jit(solution)/shard_map/all_to_all | solution.py:49
  27.5 5.0 fusion.16
  36.7 3.5 all-to-all-start.1
  41.0 15.9 %all-to-all-done.1 = bf16[8,18,1440]{2,1,0:T(8,128)(2,1)S(1)} async-done(((bf16[8,18,1440]{2,1,0:T(8,128)(2,1)}), bf16[8,18,1440]{2,1,0:T(8,128)(2,1)S(1)}, u32[]{:S(2)}, u32[]{:S(2)}) %all-to-all-start.1) | async-done | bytes 414752 | tf_op jit(solution)/shard_map/all_to_all | solution.py:51
  62.2 3.7 collective-permute-done
  67.6 3.5 all-to-all-start.2
  71.1 16.7 %all-to-all-done.2 = bf16[8,18,1440]{2,1,0:T(8,128)(2,1)S(1)} async-done(((bf16[8,18,1440]{2,1,0:T(8,128)(2,1)}), bf16[8,18,1440]{2,1,0:T(8,128)(2,1)S(1)}, u32[]{:S(2)}, u32[]{:S(2)}) %all-to-all-start.2) | async-done | bytes 414752 | tf_op jit(solution)/shard_map/all_to_all | solution.py:49
  88.0 5.0 fusion.14
  97.2 3.5 all-to-all-start.3
  101.0 16.5 %all-to-all-done.3 = bf16[8,18,1440]{2,1,0:T(8,128)(2,1)S(1)} async-done(((bf16[8,18,1440]{2,1,0:T(8,128)(2,1)}), bf16[8,18,1440]{2,1,0:T(8,128)(2,1)S(1)}, u32[]{:S(2)}, u32[]{:S(2)}) %all-to-all-start.3) | async-done | bytes 414752 | tf_op jit(solution)/shard_map/all_to_all | solution.py:51
  121.7 4.6 collective-permute-done.1
  128.1 3.7 all-to-all-start.4
  132.6 15.8 %all-to-all-done.4 = bf16[8,18,1440]{2,1,0:T(8,128)(2,1)S(1)} async-done(((bf16[8,18,1440]{2,1,0:T(8,128)(2,1)}), bf16[8,18,1440]{2,1,0:T(8,128)(2,1)S(1)}, u32[]{:S(2)}, u32[]{:S(2)}) %all-to-all-start.4) | async-done | bytes 414752 | tf_op jit(solution)/shard_map/all_to_all | solution.py:49
  148.7 5.0 fusion.12
  157.9 3.5 all-to-all-start.5
  161.9 16.3 %all-to-all-done.5 = bf16[8,18,1440]{2,1,0:T(8,128)(2,1)S(1)} async-done(((bf16[8,18,1440]{2,1,0:T(8,128)(2,1)}), bf16[8,18,1440]{2,1,0:T(8,128)(2,1)S(1)}, u32[]{:S(2)}, u32[]{:S(2)}) %all-to-all-start.5) | async-done | bytes 414752 | tf_op jit(solution)/shard_map/all_to_all | solution.py:51
  181.9 5.2 collective-permute-done.2
  188.0 19.1 %all_to_all.90 = bf16[8,18,1440]{2,1,0:T(8,128)(2,1)S(1)} all-to-all(bf16[8,18,1440]{2,1,0:T(8,128)(2,1)S(1)} %reshape.693), channel_id=1, replica_groups=mesh['section'=4,'expert'=8] {'expert'}, dimensions={0} | all-to-all | bytes 829440 | tf_op jit(solution)/shard_map/all_to_all | solution.py:49
  207.3 5.0 fusion.10
  216.5 3.5 all-to-all-start.7
  220.1 16.6 %all-to-all-done.7 = bf16[8,18,1440]{2,1,0:T(8,128)(2,1)S(1)} async-done(((bf16[8,18,1440]{2,1,0:T(8,128)(2,1)}), bf16[8,18,1440]{2,1,0:T(8,128)(2,1)S(1)}, u32[]{:S(2)}, u32[]{:S(2)}) %all-to-all-start.7) | async-done | bytes 414752 | tf_op jit(solution)/shard_map/all_to_all | solution.py:51
  240.5 5.2 collective-permute-done.3
  247.4 3.7 all-to-all-start.8
  252.0 15.8 %all-to-all-done.8 = bf16[8,18,1440]{2,1,0:T(8,128)(2,1)S(1)} async-done(((bf16[8,18,1440]{2,1,0:T(8,128)(2,1)}), bf16[8,18,1440]{2,1,0:T(8,128)(2,1)S(1)}, u32[]{:S(2)}, u32[]{:S(2)}) %all-to-all-start.8) | async-done | bytes 414752 | tf_op jit(solution)/shard_map/all_to_all | solution.py:49
  268.0 5.0 fusion.8
  277.3 3.5 all-to-all-start.9
  281.2 16.3 %all-to-all-done.9 = bf16[8,18,1440]{2,1,0:T(8,128)(2,1)S(1)} async-done(((bf16[8,18,1440]{2,1,0:T(8,128)(2,1)}), bf16[8,18,1440]{2,1,0:T(8,128)(2,1)S(1)}, u32[]{:S(2)}, u32[]{:S(2)}) %all-to-all-start.9) | async-done | bytes 414752 | tf_op jit(solution)/shard_map/all_to_all | solution.py:51
  301.2 5.2 collective-permute-done.4
  307.3 19.1 %all_to_all.91 = bf16[8,18,1440]{2,1,0:T(8,128)(2,1)S(1)} all-to-all(bf16[8,18,1440]{2,1,0:T(8,128)(2,1)S(1)} %reshape.707), channel_id=1, replica_groups=mesh['section'=4,'expert'=8] {'expert'}, dimensions={0} | all-to-all | bytes 829440 | tf_op jit(solution)/shard_map/all_to_all | solution.py:49
  326.7 5.0 fusion.6
  335.9 3.5 all-to-all-start.11
  339.4 16.6 %all-to-all-done.11 = bf16[8,18,1440]{2,1,0:T(8,128)(2,1)S(1)} async-done(((bf16[8,18,1440]{2,1,0:T(8,128)(2,1)}), bf16[8,18,1440]{2,1,0:T(8,128)(2,1)S(1)}, u32[]{:S(2)}, u32[]{:S(2)}) %all-to-all-start.11) | async-done | bytes 414752 | tf_op jit(solution)/shard_map/all_to_all | solution.py:51
  359.8 5.2 collective-permute-done.5
  366.7 3.8 all-to-all-start.12
  371.3 15.8 %all-to-all-done.12 = bf16[8,18,1440]{2,1,0:T(8,128)(2,1)S(1)} async-done(((bf16[8,18,1440]{2,1,0:T(8,128)(2,1)}), bf16[8,18,1440]{2,1,0:T(8,128)(2,1)S(1)}, u32[]{:S(2)}, u32[]{:S(2)}) %all-to-all-start.12) | async-done | bytes 414752 | tf_op jit(solution)/shard_map/all_to_all | solution.py:49
  387.4 5.0 fusion.4
  396.6 3.5 all-to-all-start.13
  400.6 16.3 %all-to-all-done.13 = bf16[8,18,1440]{2,1,0:T(8,128)(2,1)S(1)} async-done(((bf16[8,18,1440]{2,1,0:T(8,128)(2,1)}), bf16[8,18,1440]{2,1,0:T(8,128)(2,1)S(1)}, u32[]{:S(2)}, u32[]{:S(2)}) %all-to-all-start.13) | async-done | bytes 414752 | tf_op jit(solution)/shard_map/all_to_all | solution.py:51
  420.6 5.2 collective-permute-done.6
  426.7 19.1 %all_to_all.92 = bf16[8,18,1440]{2,1,0:T(8,128)(2,1)S(1)} all-to-all(bf16[8,18,1440]{2,1,0:T(8,128)(2,1)S(1)} %reshape.721), channel_id=1, replica_groups=mesh['section'=4,'expert'=8] {'expert'}, dimensions={0} | all-to-all | bytes 829440 | tf_op jit(solution)/shard_map/all_to_all | solution.py:49
  446.1 5.0 fusion.2
  458.8 16.6 %all-to-all-done.15 = bf16[8,18,1440]{2,1,0:T(8,128)(2,1)S(1)} async-done(((bf16[8,18,1440]{2,1,0:T(8,128)(2,1)}), bf16[8,18,1440]{2,1,0:T(8,128)(2,1)S(1)}, u32[]{:S(2)}, u32[]{:S(2)}) %all-to-all-start.15) | async-done | bytes 414752 | tf_op jit(solution)/shard_map/all_to_all | solution.py:51
  479.2 5.2 collective-permute-done.7
  485.3 19.4 %all_to_all.93 = bf16[8,18,1440]{2,1,0:T(8,128)(2,1)S(1)} all-to-all(bf16[8,18,1440]{2,1,0:T(8,128)(2,1)S(1)} %reshape.728), channel_id=1, replica_groups=mesh['section'=4,'expert'=8] {'expert'}, dimensions={0} | all-to-all | bytes 829440 | tf_op jit(solution)/shard_map/all_to_all | solution.py:49
  505.0 5.0 fusion
  514.2 3.5 all-to-all-start.17
  518.5 15.9 %all-to-all-done.17 = bf16[8,18,1440]{2,1,0:T(8,128)(2,1)S(1)} async-done(((bf16[8,18,1440]{2,1,0:T(8,128)(2,1)}), bf16[8,18,1440]{2,1,0:T(8,128)(2,1)S(1)}, u32[]{:S(2)}, u32[]{:S(2)}) %all-to-all-start.17) | async-done | bytes 414752 | tf_op jit(solution)/shard_map/all_to_all | solution.py:51
  (241 shorter events, 98.7 us)
Async XLA Ops:
  5.6 21.6 %all-to-all-start = ((bf16[8,18,1440]{2,1,0:T(8,128)(2,1)}), bf16[8,18,1440]{2,1,0:T(8,128)(2,1)S(1)}, u32[]{:S(2)}, u32[]{:S(2)}) async-start(bf16[8,18,1440]{2,1,0:T(8,128)(2,1)} %reshape.672), calls=%async_computation | async-start | bytes 1179648 | tf_op jit(solution)/shard_map/all_to_all | solution.py:49
  32.5 8.1 %copy-start.1 = (s32[1,6,24,4]{2,3,1,0:T(4,128)S(1)}, s32[1,6,24,4]{2,3,1,0:T(4,128)}, u32[]{:S(2)}) copy-start(s32[1,6,24,4]{2,3,1,0:T(4,128)} %param.13) | copy-start | bytes 6916
  35.8 22.9 %copy-start = (bf16[6,24,1440]{2,1,0:T(8,128)(2,1)S(1)}, bf16[6,24,1440]{2,1,0:T(8,128)(2,1)}, u32[]{:S(2)}) copy-start(bf16[6,24,1440]{2,1,0:T(8,128)(2,1)} %param.8) | copy-start | bytes 1244164
  36.7 20.2 %all-to-all-start.1 = ((bf16[8,18,1440]{2,1,0:T(8,128)(2,1)}), bf16[8,18,1440]{2,1,0:T(8,128)(2,1)S(1)}, u32[]{:S(2)}, u32[]{:S(2)}) async-start(bf16[8,18,1440]{2,1,0:T(8,128)(2,1)} %reshape.674), calls=%async_computation.1 | async-start | bytes 1179648 | tf_op jit(solution)/shard_map/all_to_all | solution.py:51
  58.8 7.1 %collective-permute-start = (bf16[24,1440]{1,0:T(8,128)(2,1)S(1)}, bf16[24,1440]{1,0:T(8,128)(2,1)S(1)}, u32[]{:S(2)}, u32[]{:S(2)}) collective-permute-start(bf16[24,1440]{1,0:T(8,128)(2,1)S(1)} %fusion.117), channel_id=1, source_target_pairs={{0,8},{8,16},{16,24},{1,9},{9,17},{17,25},{2,10},{10,18},{18,26},{... | collective-permute-start | bytes 207368 | tf_op jit(solution)/shard_map/ppermute | solution.py:10
  67.6 20.2 %all-to-all-start.2 = ((bf16[8,18,1440]{2,1,0:T(8,128)(2,1)}), bf16[8,18,1440]{2,1,0:T(8,128)(2,1)S(1)}, u32[]{:S(2)}, u32[]{:S(2)}) async-start(bf16[8,18,1440]{2,1,0:T(8,128)(2,1)} %reshape.679), calls=%async_computation.2 | async-start | bytes 1179648 | tf_op jit(solution)/shard_map/all_to_all | solution.py:49
  97.2 20.2 %all-to-all-start.3 = ((bf16[8,18,1440]{2,1,0:T(8,128)(2,1)}), bf16[8,18,1440]{2,1,0:T(8,128)(2,1)S(1)}, u32[]{:S(2)}, u32[]{:S(2)}) async-start(bf16[8,18,1440]{2,1,0:T(8,128)(2,1)} %reshape.681), calls=%async_computation.3 | async-start | bytes 1179648 | tf_op jit(solution)/shard_map/all_to_all | solution.py:51
  119.2 7.1 %collective-permute-start.1 = (bf16[24,1440]{1,0:T(8,128)(2,1)S(1)}, bf16[24,1440]{1,0:T(8,128)(2,1)S(1)}, u32[]{:S(2)}, u32[]{:S(2)}) collective-permute-start(bf16[24,1440]{1,0:T(8,128)(2,1)S(1)} %get-tuple-element.56), channel_id=1, source_target_pairs={{0,8},{8,16},{16,24},{1,9},{9,17},{17,25},{2,10},{10,18},{18,26},{... | collective-permute-start | bytes 207368 | tf_op jit(solution)/shard_map/ppermute | solution.py:10
  128.1 20.4 %all-to-all-start.4 = ((bf16[8,18,1440]{2,1,0:T(8,128)(2,1)}), bf16[8,18,1440]{2,1,0:T(8,128)(2,1)S(1)}, u32[]{:S(2)}, u32[]{:S(2)}) async-start(bf16[8,18,1440]{2,1,0:T(8,128)(2,1)} %reshape.686), calls=%async_computation.4 | async-start | bytes 1179648 | tf_op jit(solution)/shard_map/all_to_all | solution.py:49
  157.9 20.2 %all-to-all-start.5 = ((bf16[8,18,1440]{2,1,0:T(8,128)(2,1)}), bf16[8,18,1440]{2,1,0:T(8,128)(2,1)S(1)}, u32[]{:S(2)}, u32[]{:S(2)}) async-start(bf16[8,18,1440]{2,1,0:T(8,128)(2,1)} %reshape.688), calls=%async_computation.5 | async-start | bytes 1179648 | tf_op jit(solution)/shard_map/all_to_all | solution.py:51
  179.9 7.1 %collective-permute-start.2 = (bf16[24,1440]{1,0:T(8,128)(2,1)S(1)}, bf16[24,1440]{1,0:T(8,128)(2,1)S(1)}, u32[]{:S(2)}, u32[]{:S(2)}) collective-permute-start(bf16[24,1440]{1,0:T(8,128)(2,1)S(1)} %get-tuple-element.50), channel_id=1, source_target_pairs={{0,8},{8,16},{16,24},{1,9},{9,17},{17,25},{2,10},{10,18},{18,26},{... | collective-permute-start | bytes 207368 | tf_op jit(solution)/shard_map/ppermute | solution.py:10
  216.5 20.2 %all-to-all-start.7 = ((bf16[8,18,1440]{2,1,0:T(8,128)(2,1)}), bf16[8,18,1440]{2,1,0:T(8,128)(2,1)S(1)}, u32[]{:S(2)}, u32[]{:S(2)}) async-start(bf16[8,18,1440]{2,1,0:T(8,128)(2,1)} %reshape.695), calls=%async_computation.7 | async-start | bytes 1179648 | tf_op jit(solution)/shard_map/all_to_all | solution.py:51
  238.5 7.1 %collective-permute-start.3 = (bf16[24,1440]{1,0:T(8,128)(2,1)S(1)}, bf16[24,1440]{1,0:T(8,128)(2,1)S(1)}, u32[]{:S(2)}, u32[]{:S(2)}) collective-permute-start(bf16[24,1440]{1,0:T(8,128)(2,1)S(1)} %get-tuple-element.44), channel_id=1, source_target_pairs={{0,8},{8,16},{16,24},{1,9},{9,17},{17,25},{2,10},{10,18},{18,26},{... | collective-permute-start | bytes 207368 | tf_op jit(solution)/shard_map/ppermute | solution.py:10
  247.4 20.4 %all-to-all-start.8 = ((bf16[8,18,1440]{2,1,0:T(8,128)(2,1)}), bf16[8,18,1440]{2,1,0:T(8,128)(2,1)S(1)}, u32[]{:S(2)}, u32[]{:S(2)}) async-start(bf16[8,18,1440]{2,1,0:T(8,128)(2,1)} %reshape.700), calls=%async_computation.8 | async-start | bytes 1179648 | tf_op jit(solution)/shard_map/all_to_all | solution.py:49
  277.3 20.2 %all-to-all-start.9 = ((bf16[8,18,1440]{2,1,0:T(8,128)(2,1)}), bf16[8,18,1440]{2,1,0:T(8,128)(2,1)S(1)}, u32[]{:S(2)}, u32[]{:S(2)}) async-start(bf16[8,18,1440]{2,1,0:T(8,128)(2,1)} %reshape.702), calls=%async_computation.9 | async-start | bytes 1179648 | tf_op jit(solution)/shard_map/all_to_all | solution.py:51
  299.3 7.1 %collective-permute-start.4 = (bf16[24,1440]{1,0:T(8,128)(2,1)S(1)}, bf16[24,1440]{1,0:T(8,128)(2,1)S(1)}, u32[]{:S(2)}, u32[]{:S(2)}) collective-permute-start(bf16[24,1440]{1,0:T(8,128)(2,1)S(1)} %get-tuple-element.38), channel_id=1, source_target_pairs={{0,8},{8,16},{16,24},{1,9},{9,17},{17,25},{2,10},{10,18},{18,26},{... | collective-permute-start | bytes 207368 | tf_op jit(solution)/shard_map/ppermute | solution.py:10
  335.9 20.2 %all-to-all-start.11 = ((bf16[8,18,1440]{2,1,0:T(8,128)(2,1)}), bf16[8,18,1440]{2,1,0:T(8,128)(2,1)S(1)}, u32[]{:S(2)}, u32[]{:S(2)}) async-start(bf16[8,18,1440]{2,1,0:T(8,128)(2,1)} %reshape.709), calls=%async_computation.11 | async-start | bytes 1179648 | tf_op jit(solution)/shard_map/all_to_all | solution.py:51
  357.9 7.1 %collective-permute-start.5 = (bf16[24,1440]{1,0:T(8,128)(2,1)S(1)}, bf16[24,1440]{1,0:T(8,128)(2,1)S(1)}, u32[]{:S(2)}, u32[]{:S(2)}) collective-permute-start(bf16[24,1440]{1,0:T(8,128)(2,1)S(1)} %get-tuple-element.32), channel_id=1, source_target_pairs={{0,8},{8,16},{16,24},{1,9},{9,17},{17,25},{2,10},{10,18},{18,26},{... | collective-permute-start | bytes 207368 | tf_op jit(solution)/shard_map/ppermute | solution.py:10
  366.7 20.5 %all-to-all-start.12 = ((bf16[8,18,1440]{2,1,0:T(8,128)(2,1)}), bf16[8,18,1440]{2,1,0:T(8,128)(2,1)S(1)}, u32[]{:S(2)}, u32[]{:S(2)}) async-start(bf16[8,18,1440]{2,1,0:T(8,128)(2,1)} %reshape.714), calls=%async_computation.12 | async-start | bytes 1179648 | tf_op jit(solution)/shard_map/all_to_all | solution.py:49
  396.6 20.2 %all-to-all-start.13 = ((bf16[8,18,1440]{2,1,0:T(8,128)(2,1)}), bf16[8,18,1440]{2,1,0:T(8,128)(2,1)S(1)}, u32[]{:S(2)}, u32[]{:S(2)}) async-start(bf16[8,18,1440]{2,1,0:T(8,128)(2,1)} %reshape.716), calls=%async_computation.13 | async-start | bytes 1179648 | tf_op jit(solution)/shard_map/all_to_all | solution.py:51
  418.7 7.1 %collective-permute-start.6 = (bf16[24,1440]{1,0:T(8,128)(2,1)S(1)}, bf16[24,1440]{1,0:T(8,128)(2,1)S(1)}, u32[]{:S(2)}, u32[]{:S(2)}) collective-permute-start(bf16[24,1440]{1,0:T(8,128)(2,1)S(1)} %get-tuple-element.26), channel_id=1, source_target_pairs={{0,8},{8,16},{16,24},{1,9},{9,17},{17,25},{2,10},{10,18},{18,26},{... | collective-permute-start | bytes 207368 | tf_op jit(solution)/shard_map/ppermute | solution.py:10
  455.2 20.2 %all-to-all-start.15 = ((bf16[8,18,1440]{2,1,0:T(8,128)(2,1)}), bf16[8,18,1440]{2,1,0:T(8,128)(2,1)S(1)}, u32[]{:S(2)}, u32[]{:S(2)}) async-start(bf16[8,18,1440]{2,1,0:T(8,128)(2,1)} %reshape.723), calls=%async_computation.15 | async-start | bytes 1179648 | tf_op jit(solution)/shard_map/all_to_all | solution.py:51
  477.3 7.1 %collective-permute-start.7 = (bf16[24,1440]{1,0:T(8,128)(2,1)S(1)}, bf16[24,1440]{1,0:T(8,128)(2,1)S(1)}, u32[]{:S(2)}, u32[]{:S(2)}) collective-permute-start(bf16[24,1440]{1,0:T(8,128)(2,1)S(1)} %get-tuple-element.20), channel_id=1, source_target_pairs={{0,8},{8,16},{16,24},{1,9},{9,17},{17,25},{2,10},{10,18},{18,26},{... | collective-permute-start | bytes 207368 | tf_op jit(solution)/shard_map/ppermute | solution.py:10
  514.2 20.2 %all-to-all-start.17 = ((bf16[8,18,1440]{2,1,0:T(8,128)(2,1)}), bf16[8,18,1440]{2,1,0:T(8,128)(2,1)S(1)}, u32[]{:S(2)}, u32[]{:S(2)}) async-start(bf16[8,18,1440]{2,1,0:T(8,128)(2,1)} %reshape.730), calls=%async_computation.17 | async-start | bytes 1179648 | tf_op jit(solution)/shard_map/all_to_all | solution.py:51
where the time goes:
time: 548 us; the launch traced here: 537 us
  waiting for transfers between devices  267 us (49%)
  blocking collectives  76.9 us (14%)
  matrix products  76.4 us (14%)
  starting transfers between devices  68.9 us (13%)
  local copies, waits for them, and re-layouts  34.8 us (6%)
  other arithmetic  11.4 us (2%)
    all_to_all x9, waiting for transfers between devices, layer_step(): lax.all_to_all(computed, 'expert', split_axis=0, concat_axis=0, tiled=True)  147 us
    all_to_all x5, waiting for transfers between devices, layer_step(): lax.all_to_all(outgoing, 'expert', split_axis=0, concat_axis=0, tiled=True)  80.4 us
    all_to_all x4, blocking collectives, layer_step(): lax.all_to_all(outgoing, 'expert', split_axis=0, concat_axis=0, tiled=True)  76.9 us
    dot_general x9, matrix products, expert_ffn(): jnp.dot(flat_rows, gate_up_w, preferred_element_type=jnp.float32)  44.8 us
    ppermute x8, waiting for transfers between devices, passed_along(): lax.ppermute(value, axis, [(source, source + steps) for source in range(l...  39.6 us
    all_to_all x9, starting transfers between devices, layer_step(): lax.all_to_all(computed, 'expert', split_axis=0, concat_axis=0, tiled=True)  31.8 us
    dot_general x9, matrix products, expert_ffn(): jnp.dot(activated, down_w, preferred_element_type=jnp.float32)  29.3 us
    all_to_all x5, starting transfers between devices, layer_step(): lax.all_to_all(outgoing, 'expert', split_axis=0, concat_axis=0, tiled=True)  19.7 us
  transfers between devices with their start and end apart: 22, of which 22 were waited for; matrix products, arithmetic and copies ran while one was open for 1% of the time, Pallas kernels for 0%

commit v1 on v0

--- a/solution.py
+++ b/solution.py
@@ -1,7 +1,18 @@
+import functools
+
 import jax
 import jax.numpy as jnp
 from jax import lax
+from jax.experimental import pallas as pl
+from jax.experimental.pallas import tpu as pltpu
 from jax.sharding import PartitionSpec as P
+
+F32 = jnp.float32
+BF16 = jnp.bfloat16
+LANES = 128
+CORES = 2
+CHUNK = 256
+VMEM_BYTES = 56 * 2**20
 
 
 def passed_along(value, axis, steps):
@@ -61,7 +72,7 @@
     return accumulated.astype(jnp.bfloat16)
 
 
-def shards(tokens, norm_gain, gate_up, down, routes, route_weights):
+def ticked_shards(tokens, norm_gain, gate_up, down, routes, route_weights):
     micro_count, token_count, width = tokens.shape
     sections = lax.axis_size("section")
     section_index = lax.axis_index("section")
@@ -87,7 +98,335 @@
     return results[None]
 
 
+def folded(rows, half):
+    token_count, width = rows.shape
+    rest = jnp.concatenate(
+        [rows[:, half:], jnp.zeros((token_count, 2 * half - width), rows.dtype)], axis=1
+    )
+    return jnp.concatenate([rows[:, :half], rest], axis=0)
+
+
+def kernel(
+    dims,
+    tokens_ref, gain_ref, gate_up_hbm, down_hbm, routes_ref, weights_ref,
+    out_ref,
+    gate_up_w, up_w, down_w, stream, blocks, rows_x, rows_act, partial, sib_out, sib_in,
+    sum_out, sum_in, passed,
+    weight_sem, lane_send, lane_recv, fwd_send, sib_send, sib_recv, sum_send, sum_recv,
+    pass_send, pass_recv,
+):
+    sections, experts, micros, token_count, width, hidden, half = dims
+    chips = experts // CORES
+    second = width - half
+    tile = second // LANES * LANES
+    spot = second - tile
+    section, me = lax.axis_index("section"), lax.axis_index("expert")
+    chip, core = me // CORES, me % CORES
+    sibling = chip * CORES + 1 - core
+
+    loads = [
+        pltpu.make_async_copy(gate_up_hbm.at[0, 0], gate_up_w, weight_sem.at[0]),
+        pltpu.make_async_copy(down_hbm.at[0, 0], down_w, weight_sem.at[1]),
+    ]
+    for load in loads:
+        load.start()
+
+    def other(step):
+        return lax.rem(chip + step, chips)
+
+    def to(src, dst, send, recv, expert, sec=section):
+        return pltpu.make_async_remote_copy(
+            src_ref=src, dst_ref=dst, send_sem=send, recv_sem=recv,
+            device_id=(sec, expert), device_id_type=pl.DeviceIdType.MESH,
+        )
+
+    barrier = pltpu.get_barrier_semaphore()
+    for step in range(1, chips):
+        pl.semaphore_signal(
+            barrier, inc=1, device_id=(section, other(step) * CORES + core),
+            device_id_type=pl.DeviceIdType.MESH,
+        )
+    pl.semaphore_signal(
+        barrier, inc=1, device_id=(section, sibling), device_id_type=pl.DeviceIdType.MESH
+    )
+
+    @pl.when(section > 0)
+    def _():
+        pl.semaphore_signal(
+            barrier, inc=1, device_id=(section - 1, me), device_id_type=pl.DeviceIdType.MESH
+        )
+
+    pl.semaphore_wait(barrier, chips + jnp.where(section + 1 < sections, 1, 0))
+
+    @pl.when(section == 0)
+    def _():
+        for m in range(micros):
+            stream[m] = folded(tokens_ref[m].astype(F32), half).astype(BF16)
+
+    gain = folded(gain_ref[...], half)
+
+    def lane_copy(m, step):
+        return to(
+            blocks.at[m, me], blocks.at[m, me], lane_send.at[m, step], lane_recv.at[m, me],
+            other(step) * CORES + core,
+        )
+
+    def sibling_copy(m, owner, step):
+        return to(
+            blocks.at[m, owner], blocks.at[m, owner], fwd_send.at[m, step],
+            lane_recv.at[m, owner], sibling,
+        )
+
+    def partial_copy(m):
+        return to(sib_out.at[m], sib_in.at[m], sib_send.at[m], sib_recv.at[m], sibling)
+
+    def sum_copy(m, step):
+        there = other(step)
+        return to(
+            sum_out.at[m, there], sum_in.at[m, chip], sum_send.at[m, step],
+            sum_recv.at[m, chip], there * CORES + core,
+        )
+
+    def pass_copy(m):
+        return to(
+            passed.at[m], stream.at[m], pass_send.at[m], pass_recv.at[m], me,
+            lax.rem(section + 1, sections),
+        )
+
+    def got_block(m, owner):
+        to(
+            blocks.at[m, owner], blocks.at[m, owner], fwd_send.at[m, 0],
+            lane_recv.at[m, owner], sibling,
+        ).wait_recv()
+
+    def send_rows(m):
+        @pl.when(section > 0)
+        def _():
+            pass_copy(m).wait_recv()
+
+        both = stream[m].astype(F32)
+        low, high = both[:token_count], both[token_count:]
+        squares = jnp.sum(low * low, axis=-1, keepdims=True) + jnp.sum(
+            high * high, axis=-1, keepdims=True
+        )
+        scale = lax.rsqrt(squares / width + 1e-05)
+        low = low * scale * gain[:1]
+        high = high * scale * gain[1:]
+        route_rows = routes_ref[0, m]
+        fixed_point = weights_ref[0, m].astype(F32)
+        shares = fixed_point / jnp.sum(fixed_point, axis=-1, keepdims=True)
+        lane = lax.broadcasted_iota(jnp.int32, (token_count, LANES), 1) - spot
+        first = jnp.zeros((token_count, LANES), F32)
+        again = jnp.zeros((token_count, LANES), F32)
+        for k in range(route_rows.shape[1]):
+            named, share = route_rows[:, k : k + 1], shares[:, k : k + 1]
+            first = first + jnp.where(named == lane, share, 0.0)
+            again = again + jnp.where(named == lane - experts, share, 0.0)
+        rest = again - again.astype(BF16).astype(F32)
+        last = high[:, tile:] + first + rest
+        high = last if tile == 0 else jnp.concatenate([high[:, :tile], last], axis=1)
+        blocks[m, me] = jnp.concatenate([low, high], axis=0).astype(BF16)
+        for step in range(1, chips):
+            lane_copy(m, step).start()
+        sibling_copy(m, me, 0).start()
+
+    def forward_rows(m):
+        for step in range(1, chips):
+            owner = other(step) * CORES + core
+            got_block(m, owner)
+            sibling_copy(m, owner, step).start()
+
+    def compute(m):
+        for step in range(chips):
+            got_block(m, other(step) * CORES + 1 - core)
+        rows = experts * token_count
+        arrived = blocks[m].astype(F32)
+        low = arrived[:, :token_count].reshape(rows, half)
+        high = arrived[:, token_count:].reshape(rows, half)
+        lane = lax.broadcasted_iota(jnp.int32, (rows, LANES), 1) - spot
+        mine = jnp.logical_or(lane == me, lane == me + experts)
+        share = jnp.sum(jnp.where(mine, high[:, tile:], 0.0), axis=-1, keepdims=True)
+        rows_x[:, :half] = low.astype(BF16)
+        rows_x[:, half:] = high.astype(BF16)
+        x = rows_x[:, :width]
+        for at in range(0, hidden, CHUNK):
+            upto = min(at + CHUNK, hidden)
+            gate = jnp.dot(x, gate_up_w[:, at:upto], preferred_element_type=F32)
+            up = jnp.dot(x, up_w[:, at:upto], preferred_element_type=F32)
+            rows_act[:, at:upto] = (gate * jax.nn.sigmoid(1.702 * gate) * (up + 1.0)).astype(BF16)
+        act = rows_act[:, :hidden]
+        for at in [*range(0, half, CHUNK), *range(half, width, CHUNK)]:
+            end = half if at < half else 2 * half
+            room = min(CHUNK, end - at)
+            upto = min(at + room, width)
+            value = jnp.dot(act, down_w[:, at:upto], preferred_element_type=F32) * share
+            if upto - at < room:
+                value = jnp.concatenate(
+                    [value, jnp.zeros((rows, room - (upto - at)), F32)], axis=1
+                )
+            value = value.reshape(chips, CORES, token_count, room)
+            top = 0 if at < half else token_count
+            left = at if at < half else at - half
+            for c in range(CORES):
+                partial[c, :, top : top + token_count, left : left + room] = value[:, c]
+
+    def add_siblings(m):
+        sib_out[m] = partial[1 - core].astype(BF16)
+        partial_copy(m).start()
+
+    def send_sums(m):
+        partial_copy(m).wait_recv()
+        for step in range(chips - 1, 0, -1):
+            there = other(step)
+            total = partial[core, there] + sib_in[m, there].astype(F32)
+            sum_out[m, there] = total.astype(BF16)
+            sum_copy(m, step).start()
+
+    def finish(m):
+        total = stream[m].astype(F32) + partial[core, chip] + sib_in[m, chip].astype(F32)
+        for step in range(1, chips):
+            there = other(step)
+            to(
+                sum_out.at[m, there], sum_in.at[m, there], sum_send.at[m, step],
+                sum_recv.at[m, there], there * CORES + core,
+            ).wait_recv()
+            total = total + sum_in[m, there].astype(F32)
+        passed[m] = total.astype(BF16)
+
+        @pl.when(section + 1 < sections)
+        def _():
+            pass_copy(m).start()
+
+        out_ref[0, m] = jnp.concatenate(
+            [total[:token_count], total[token_count:, :second]], axis=1
+        ).astype(BF16)
+
+    send_rows(0)
+    loads[0].wait()
+
+    def realign(i, carry):
+        at = pl.ds(pl.multiple_of(i * 32, 32), 32)
+        up_w[at, :] = gate_up_w[at, hidden:]
+        return carry
+
+    lax.fori_loop(0, width // 32, realign, 0)
+    loads[1].wait()
+    forward_rows(0)
+
+    def step_over(m, carry):
+        compute(m)
+        add_siblings(m)
+        send_sums(m)
+
+        @pl.when(m + 1 < micros)
+        def _():
+            send_rows(m + 1)
+
+        finish(m)
+
+        @pl.when(m + 1 < micros)
+        def _():
+            forward_rows(m + 1)
+
+        return carry
+
+    lax.fori_loop(0, micros, step_over, 0)
+
+    def drain(m, carry):
+        for step in range(1, chips):
+            lane_copy(m, step).wait_send()
+            sum_copy(m, step).wait_send()
+        for step in range(chips):
+            sibling_copy(m, me, step).wait_send()
+        partial_copy(m).wait_send()
+
+        @pl.when(section + 1 < sections)
+        def _():
+            pass_copy(m).wait_send()
+
+        return carry
+
+    lax.fori_loop(0, micros, drain, 0)
+
+
+def half_width(width):
+    tiles = -(-width // LANES)
+    return -(-tiles // 2) * LANES
+
+
+def fits_vmem(sections, experts, micros, token_count, width, hidden):
+    half = half_width(width)
+    chips = experts // CORES
+    block = 2 * token_count * half * 2
+    held = micros * block * (experts + 3 * chips + 3) + 2 * experts * block
+    held += (2 * hidden + 4 * LANES) * width * 4
+    room = (width - half) % LANES + 2 * experts <= LANES and width < 2 * half
+    rows_ok = token_count % 8 == 0 and width % 32 == 0 and hidden % 32 == 0
+    return experts % CORES == 0 and experts > CORES and room and rows_ok and held < 32 * 2**20
+
+
+def whole_kernel(tokens, norm_gain, gate_up, down, routes, route_weights):
+    micros, token_count, width = tokens.shape
+    hidden = down.shape[2]
+    sections, experts = lax.axis_size("section"), lax.axis_size("expert")
+    half = half_width(width)
+    chips = experts // CORES
+    dims = (sections, experts, micros, token_count, width, hidden, half)
+    folded_rows = 2 * token_count
+    rows = experts * token_count
+    dma = pltpu.SemaphoreType.DMA
+    vmem = pl.BlockSpec(memory_space=pltpu.VMEM)
+    hbm = pl.BlockSpec(memory_space=pl.ANY)
+    work = 6 * micros * rows * width * hidden
+    return pl.pallas_call(
+        functools.partial(kernel, dims),
+        out_shape=jax.ShapeDtypeStruct((1, micros, token_count, width), BF16),
+        in_specs=[vmem, vmem, hbm, hbm, vmem, vmem],
+        out_specs=vmem,
+        scratch_shapes=[
+            pltpu.VMEM((width, 2 * hidden), BF16),
+            pltpu.VMEM((width, hidden), BF16),
+            pltpu.VMEM((hidden, width), BF16),
+            pltpu.VMEM((micros, folded_rows, half), BF16),
+            pltpu.VMEM((micros, experts, folded_rows, half), BF16),
+            pltpu.VMEM((rows, 2 * half), BF16),
+            pltpu.VMEM((rows, hidden), BF16),
+            pltpu.VMEM((CORES, chips, folded_rows, half), F32),
+            pltpu.VMEM((micros, chips, folded_rows, half), BF16),
+            pltpu.VMEM((micros, chips, folded_rows, half), BF16),
+            pltpu.VMEM((micros, chips, folded_rows, half), BF16),
+            pltpu.VMEM((micros, chips, folded_rows, half), BF16),
+            pltpu.VMEM((micros, folded_rows, half), BF16),
+            dma((2,)),
+            dma((micros, chips)),
+            dma((micros, experts)),
+            dma((micros, chips)),
+            dma((micros,)),
+            dma((micros,)),
+            dma((micros, chips)),
+            dma((micros, chips)),
+            dma((micros,)),
+            dma((micros,)),
+        ],
+        compiler_params=pltpu.CompilerParams(
+            collective_id=0, has_side_effects=True, vmem_limit_bytes=VMEM_BYTES
+        ),
+        cost_estimate=pl.CostEstimate(
+            flops=work, bytes_accessed=6 * width * hidden, transcendentals=micros * rows * hidden
+        ),
+    )(tokens, norm_gain, gate_up, down, routes, route_weights)
+
+
 def solution(mesh):
+    sections, experts = mesh.shape["section"], mesh.shape["expert"]
+
+    def shards(tokens, norm_gain, gate_up, down, routes, route_weights):
+        micros, token_count, width = tokens.shape
+        hidden = down.shape[2]
+        if fits_vmem(sections, experts, micros, token_count, width, hidden):
+            return whole_kernel(tokens, norm_gain, gate_up, down, routes, route_weights)
+        return ticked_shards(tokens, norm_gain, gate_up, down, routes, route_weights)
+
     return jax.shard_map(
         shards,
         mesh=mesh,

time: 548 us -> 199 us (0.36)
  the two profiles are of different devices: /device:TPU:4 before, /device:TPU:23 now
where the time goes in v1:
time: 199 us; the launch traced here: 198 us
  Pallas kernels  194 us (97%)
  local copies, waits for them, and re-layouts  4.69 us (2%)
    pallas_call x1, Pallas kernels, whole_kernel(): pl.pallas_call(functools.partial(kernel, dims), out_shape=jax.ShapeDtypeS...  194 us
    unnamed x3, local copies, waits for them, and re-layouts  4.69 us

profile of v1, /device:TPU:23, one launch (start us, length us, event | category | flops | bytes accessed | tf_op | source)
XLA Modules:
  0.0 198.4 jit_solution(8671923949921040979)
XLA Ops:
  0.0 1.4 copy.7.routes_ref
  1.4 1.4 copy.8.weights_ref
  2.9 193.7 %shard_map.64 = bf16[1,6,24,1440]{3,2,1,0:T(8,128)(2,1)} custom-call(bf16[6,24,1440]{2,1,0:T(8,128)(2,1)} %tokens_ref.1, f32[1,1440]{1,0:T(1,128)} %gain_ref.1, bf16[1,1,1440,2880]{3,2,1,0:T(8,128)(2,1)} %gate_up_hbm.1, bf16[1,1,1440,1440]{3,2,1,0:T(8,128)(2,1)} %down_hbm.1, s32[1,6,24,4]{3,2,1,0:T(8,128)} %copy.7.routes_ref, s32[1,6,24,4]{3,2,1,0:T(8,128)} %copy.8.weights_ref), custom_call_target="tpu_custom_call" | custom-call | flops 14332723200 | bytes 12441600 | tf_op jit(solution)/shard_map/pallas_call | solution.py:381
  196.6 1.8 copy.10

commit v2 on v1

--- a/solution.py
+++ b/solution.py
@@ -111,8 +111,8 @@
     tokens_ref, gain_ref, gate_up_hbm, down_hbm, routes_ref, weights_ref,
     out_ref,
     gate_up_w, up_w, down_w, stream, blocks, rows_x, rows_act, partial, sib_out, sib_in,
-    sum_out, sum_in, passed,
-    weight_sem, lane_send, lane_recv, fwd_send, sib_send, sib_recv, sum_send, sum_recv,
+    sum_out, sum_in, passed, share_lanes,
+    weight_sem, up_send, low_send, lane_recv, fwd_send, sib_send, sib_recv, sum_send, sum_recv,
     pass_send, pass_recv,
 ):
     sections, experts, micros, token_count, width, hidden, half = dims
@@ -165,20 +165,31 @@
 
     gain = folded(gain_ref[...], half)
 
-    def lane_copy(m, step):
+    def up_copy(m, hop):
+        owner = (chip - hop) * CORES + core
         return to(
-            blocks.at[m, me], blocks.at[m, me], lane_send.at[m, step], lane_recv.at[m, me],
-            other(step) * CORES + core,
-        )
-
-    def sibling_copy(m, owner, step):
+            blocks.at[m, owner], blocks.at[m, owner], up_send.at[m, hop],
+            lane_recv.at[m, owner], me + CORES,
+        )
+
+    def low_copy(m, hop):
+        owner = (chip + hop) * CORES + core
         return to(
-            blocks.at[m, owner], blocks.at[m, owner], fwd_send.at[m, step],
+            blocks.at[m, owner], blocks.at[m, owner], low_send.at[m, hop],
+            lane_recv.at[m, owner], me - CORES,
+        )
+
+    def sibling_copy(m, owner):
+        return to(
+            blocks.at[m, owner], blocks.at[m, owner], fwd_send.at[m, owner // CORES],
             lane_recv.at[m, owner], sibling,
         )
 
-    def partial_copy(m):
-        return to(sib_out.at[m], sib_in.at[m], sib_send.at[m], sib_recv.at[m], sibling)
+    def partial_copy(m, part):
+        return to(
+            sib_out.at[m, part], sib_in.at[m, part], sib_send.at[m, part],
+            sib_recv.at[m, part], sibling,
+        )
 
     def sum_copy(m, step):
         there = other(step)
@@ -194,10 +205,28 @@
         )
 
     def got_block(m, owner):
-        to(
-            blocks.at[m, owner], blocks.at[m, owner], fwd_send.at[m, 0],
-            lane_recv.at[m, owner], sibling,
-        ).wait_recv()
+        sibling_copy(m, owner).wait_recv()
+
+    def prepare_shares(m):
+        route_rows = routes_ref[0, m]
+        fixed_point = weights_ref[0, m].astype(F32)
+        shares = fixed_point / jnp.sum(fixed_point, axis=0, keepdims=True)
+        lane = lax.broadcasted_iota(jnp.int32, (token_count, LANES), 1) - spot
+        square = (token_count, token_count)
+        same = lax.broadcasted_iota(jnp.int32, square, 0) == lax.broadcasted_iota(
+            jnp.int32, square, 1
+        )
+        first = jnp.zeros((token_count, LANES), F32)
+        again = jnp.zeros((token_count, LANES), F32)
+        for k in range(route_rows.shape[0]):
+            named = jnp.sum(
+                jnp.where(same, route_rows[k : k + 1].astype(F32), 0.0), axis=1, keepdims=True
+            ).astype(jnp.int32)
+            share = jnp.sum(jnp.where(same, shares[k : k + 1], 0.0), axis=1, keepdims=True)
+            first = first + jnp.where(named == lane, share, 0.0)
+            again = again + jnp.where(named == lane - experts, share, 0.0)
+        rest = again - again.astype(BF16).astype(F32)
+        share_lanes[m] = first + rest
 
     def send_rows(m):
         @pl.when(section > 0)
@@ -212,31 +241,47 @@
         scale = lax.rsqrt(squares / width + 1e-05)
         low = low * scale * gain[:1]
         high = high * scale * gain[1:]
-        route_rows = routes_ref[0, m]
-        fixed_point = weights_ref[0, m].astype(F32)
-        shares = fixed_point / jnp.sum(fixed_point, axis=-1, keepdims=True)
-        lane = lax.broadcasted_iota(jnp.int32, (token_count, LANES), 1) - spot
-        first = jnp.zeros((token_count, LANES), F32)
-        again = jnp.zeros((token_count, LANES), F32)
-        for k in range(route_rows.shape[1]):
-            named, share = route_rows[:, k : k + 1], shares[:, k : k + 1]
-            first = first + jnp.where(named == lane, share, 0.0)
-            again = again + jnp.where(named == lane - experts, share, 0.0)
-        rest = again - again.astype(BF16).astype(F32)
-        last = high[:, tile:] + first + rest
+        last = high[:, tile:] + share_lanes[m]
         high = last if tile == 0 else jnp.concatenate([high[:, :tile], last], axis=1)
         blocks[m, me] = jnp.concatenate([low, high], axis=0).astype(BF16)
-        for step in range(1, chips):
-            lane_copy(m, step).start()
-        sibling_copy(m, me, 0).start()
-
-    def forward_rows(m):
-        for step in range(1, chips):
-            owner = other(step) * CORES + core
+        pass_block(m, 0)
+
+    def pass_block(m, hop):
+        @pl.when(jnp.logical_and(chip >= hop, chip + 1 < chips))
+        def _():
+            up_copy(m, hop).start()
+
+        @pl.when(jnp.logical_and(chip + hop < chips, chip > 0))
+        def _():
+            low_copy(m, hop).start()
+
+        if hop == 0:
+            sibling_copy(m, me).start()
+
+    def relay(m, hop):
+        @pl.when(chip >= hop)
+        def _():
+            owner = (chip - hop) * CORES + core
             got_block(m, owner)
-            sibling_copy(m, owner, step).start()
-
-    def compute(m):
+
+            @pl.when(chip + 1 < chips)
+            def _():
+                up_copy(m, hop).start()
+
+            sibling_copy(m, owner).start()
+
+        @pl.when(chip + hop < chips)
+        def _():
+            owner = (chip + hop) * CORES + core
+            got_block(m, owner)
+
+            @pl.when(chip > 0)
+            def _():
+                low_copy(m, hop).start()
+
+            sibling_copy(m, owner).start()
+
+    def project(m, between):
         for step in range(chips):
             got_block(m, other(step) * CORES + 1 - core)
         rows = experts * token_count
@@ -254,10 +299,16 @@
             gate = jnp.dot(x, gate_up_w[:, at:upto], preferred_element_type=F32)
             up = jnp.dot(x, up_w[:, at:upto], preferred_element_type=F32)
             rows_act[:, at:upto] = (gate * jax.nn.sigmoid(1.702 * gate) * (up + 1.0)).astype(BF16)
+            if at <= hidden // 3 < upto:
+                between()
+        return share
+
+    def bring_down(m, part, share):
         act = rows_act[:, :hidden]
-        for at in [*range(0, half, CHUNK), *range(half, width, CHUNK)]:
-            end = half if at < half else 2 * half
-            room = min(CHUNK, end - at)
+        rows = experts * token_count
+        for left in range(0, half, CHUNK):
+            at = part * half + left
+            room = min(CHUNK, half - left)
             upto = min(at + room, width)
             value = jnp.dot(act, down_w[:, at:upto], preferred_element_type=F32) * share
             if upto - at < room:
@@ -265,25 +316,26 @@
                     [value, jnp.zeros((rows, room - (upto - at)), F32)], axis=1
                 )
             value = value.reshape(chips, CORES, token_count, room)
-            top = 0 if at < half else token_count
-            left = at if at < half else at - half
             for c in range(CORES):
-                partial[c, :, top : top + token_count, left : left + room] = value[:, c]
-
-    def add_siblings(m):
-        sib_out[m] = partial[1 - core].astype(BF16)
-        partial_copy(m).start()
+                partial[c, part, :, left : left + room] = value[:, c].reshape(-1, room)
+        sib_out[m, part] = partial[1 - core, part].astype(BF16)
+        partial_copy(m, part).start()
+
+    def own_sum(there):
+        at = pl.ds(pl.multiple_of(there * token_count, 8), token_count)
+        return jnp.concatenate([partial[core, 0, at, :], partial[core, 1, at, :]], axis=0)
 
     def send_sums(m):
-        partial_copy(m).wait_recv()
+        for part in range(2):
+            partial_copy(m, part).wait_recv()
+            partial[core, part] = partial[core, part] + sib_in[m, part].astype(F32)
         for step in range(chips - 1, 0, -1):
             there = other(step)
-            total = partial[core, there] + sib_in[m, there].astype(F32)
-            sum_out[m, there] = total.astype(BF16)
+            sum_out[m, there] = own_sum(there).astype(BF16)
             sum_copy(m, step).start()
 
     def finish(m):
-        total = stream[m].astype(F32) + partial[core, chip] + sib_in[m, chip].astype(F32)
+        total = stream[m].astype(F32) + own_sum(chip)
         for step in range(1, chips):
             there = other(step)
             to(
@@ -301,7 +353,13 @@
             [total[:token_count], total[token_count:, :second]], axis=1
         ).astype(BF16)
 
+    def prepare(m, carry):
+        prepare_shares(m)
+        return carry
+
+    prepare_shares(0)
     send_rows(0)
+    lax.fori_loop(1, micros, prepare, 0)
     loads[0].wait()
 
     def realign(i, carry):
@@ -311,34 +369,47 @@
 
     lax.fori_loop(0, width // 32, realign, 0)
     loads[1].wait()
-    forward_rows(0)
+    for hop in range(1, chips):
+        relay(0, hop)
 
     def step_over(m, carry):
-        compute(m)
-        add_siblings(m)
+        def ahead(work):
+            pl.when(m + 1 < micros)(work)
+
+        share = project(m, lambda: ahead(lambda: send_rows(m + 1)))
+
+        @pl.when(m > 0)
+        def _():
+            finish(m - 1)
+
+        bring_down(m, 0, share)
+        ahead(lambda: relay(m + 1, 1))
+        bring_down(m, 1, share)
+        if chips > 2:
+            ahead(lambda: relay(m + 1, 2))
         send_sums(m)
-
-        @pl.when(m + 1 < micros)
-        def _():
-            send_rows(m + 1)
-
-        finish(m)
-
-        @pl.when(m + 1 < micros)
-        def _():
-            forward_rows(m + 1)
-
+        for hop in range(3, chips):
+            ahead(functools.partial(relay, m + 1, hop))
         return carry
 
     lax.fori_loop(0, micros, step_over, 0)
+    finish(micros - 1)
 
     def drain(m, carry):
+        for hop in range(chips):
+            @pl.when(jnp.logical_and(chip >= hop, chip + 1 < chips))
+            def _():
+                up_copy(m, hop).wait_send()
+
+            @pl.when(jnp.logical_and(chip + hop < chips, chip > 0))
+            def _():
+                low_copy(m, hop).wait_send()
+
+            sibling_copy(m, hop * CORES + core).wait_send()
         for step in range(1, chips):
-            lane_copy(m, step).wait_send()
             sum_copy(m, step).wait_send()
-        for step in range(chips):
-            sibling_copy(m, me, step).wait_send()
-        partial_copy(m).wait_send()
+        for part in range(2):
+            partial_copy(m, part).wait_send()
 
         @pl.when(section + 1 < sections)
         def _():
@@ -361,7 +432,7 @@
     held = micros * block * (experts + 3 * chips + 3) + 2 * experts * block
     held += (2 * hidden + 4 * LANES) * width * 4
     room = (width - half) % LANES + 2 * experts <= LANES and width < 2 * half
-    rows_ok = token_count % 8 == 0 and width % 32 == 0 and hidden % 32 == 0
+    rows_ok = token_count % 8 == 0 and chips * token_count % 16 == 0 and width % 32 == 0 and hidden % 32 == 0
     return experts % CORES == 0 and experts > CORES and room and rows_ok and held < 32 * 2**20
 
 
@@ -391,18 +462,20 @@
             pltpu.VMEM((micros, experts, folded_rows, half), BF16),
             pltpu.VMEM((rows, 2 * half), BF16),
             pltpu.VMEM((rows, hidden), BF16),
-            pltpu.VMEM((CORES, chips, folded_rows, half), F32),
-            pltpu.VMEM((micros, chips, folded_rows, half), BF16),
-            pltpu.VMEM((micros, chips, folded_rows, half), BF16),
+            pltpu.VMEM((CORES, 2, chips * token_count, half), F32),
+            pltpu.VMEM((micros, 2, chips * token_count, half), BF16),
+            pltpu.VMEM((micros, 2, chips * token_count, half), BF16),
             pltpu.VMEM((micros, chips, folded_rows, half), BF16),
             pltpu.VMEM((micros, chips, folded_rows, half), BF16),
             pltpu.VMEM((micros, folded_rows, half), BF16),
+            pltpu.VMEM((micros, token_count, LANES), F32),
             dma((2,)),
+            dma((micros, chips)),
             dma((micros, chips)),
             dma((micros, experts)),
             dma((micros, chips)),
-            dma((micros,)),
-            dma((micros,)),
+            dma((micros, 2)),
+            dma((micros, 2)),
             dma((micros, chips)),
             dma((micros, chips)),
             dma((micros,)),
@@ -414,7 +487,7 @@
         cost_estimate=pl.CostEstimate(
             flops=work, bytes_accessed=6 * width * hidden, transcendentals=micros * rows * hidden
         ),
-    )(tokens, norm_gain, gate_up, down, routes, route_weights)
+    )(tokens, norm_gain, gate_up, down, routes.swapaxes(2, 3), route_weights.swapaxes(2, 3))
 
 
 def solution(mesh):

time: 199 us -> 209 us (1.050)
  Pallas kernels: 194 us -> 205 us
  local copies, waits for them, and re-layouts: 4.69 us -> 1.8 us
    pallas_call x1, Pallas kernels: 194 us -> 205 us  [whole_kernel(): pl.pallas_call(functools.partial(kernel, dims), out_shape=jax.ShapeDtypeS...]
    unnamed x3 -> x1, local copies, waits for them, and re-layouts: 4.69 us -> 1.8 us
where the time goes in v2:
time: 209 us; the launch traced here: 207 us
  Pallas kernels  205 us (98%)
    pallas_call x1, Pallas kernels, whole_kernel(): pl.pallas_call(functools.partial(kernel, dims), out_shape=jax.ShapeDtypeS...  205 us

profile of v2, /device:TPU:23, one launch (start us, length us, event | category | flops | bytes accessed | tf_op | source)
XLA Modules:
  0.0 206.8 jit_solution(5839608486924738007)
XLA Ops:
  0.0 205.0 %shard_map.64 = bf16[1,6,24,1440]{3,2,1,0:T(8,128)(2,1)} custom-call(bf16[6,24,1440]{2,1,0:T(8,128)(2,1)} %tokens_ref.1, f32[1,1440]{1,0:T(1,128)} %gain_ref.1, bf16[1,1,1440,2880]{3,2,1,0:T(8,128)(2,1)} %gate_up_hbm.1, bf16[1,1,1440,1440]{3,2,1,0:T(8,128)(2,1)} %down_hbm.1, s32[1,6,4,24]{3,2,1,0:T(4,128)} %bitcast.2, s32[1,6,4,24]{3,2,1,0:T(4,128)} %bitcast.3), custom_call_target="tpu_custom_call" | custom-call | flops 14332723200 | bytes 12441600 | tf_op jit(solution)/shard_map/pallas_call | solution.py:452
  205.0 1.8 copy.8

commit v3 on v2

--- a/solution.py
+++ b/solution.py
@@ -281,7 +281,7 @@
 
             sibling_copy(m, owner).start()
 
-    def project(m, between):
+    def project(m):
         for step in range(chips):
             got_block(m, other(step) * CORES + 1 - core)
         rows = experts * token_count
@@ -299,8 +299,6 @@
             gate = jnp.dot(x, gate_up_w[:, at:upto], preferred_element_type=F32)
             up = jnp.dot(x, up_w[:, at:upto], preferred_element_type=F32)
             rows_act[:, at:upto] = (gate * jax.nn.sigmoid(1.702 * gate) * (up + 1.0)).astype(BF16)
-            if at <= hidden // 3 < upto:
-                between()
         return share
 
     def bring_down(m, part, share):
@@ -358,7 +356,11 @@
         return carry
 
     prepare_shares(0)
-    send_rows(0)
+
+    @pl.when(section == 0)
+    def _():
+        send_rows(0)
+
     lax.fori_loop(1, micros, prepare, 0)
     loads[0].wait()
 
@@ -369,31 +371,34 @@
 
     lax.fori_loop(0, width // 32, realign, 0)
     loads[1].wait()
+
+    @pl.when(section > 0)
+    def _():
+        send_rows(0)
+
     for hop in range(1, chips):
         relay(0, hop)
 
     def step_over(m, carry):
-        def ahead(work):
-            pl.when(m + 1 < micros)(work)
-
-        share = project(m, lambda: ahead(lambda: send_rows(m + 1)))
-
-        @pl.when(m > 0)
-        def _():
-            finish(m - 1)
-
-        bring_down(m, 0, share)
-        ahead(lambda: relay(m + 1, 1))
-        bring_down(m, 1, share)
-        if chips > 2:
-            ahead(lambda: relay(m + 1, 2))
+        share = project(m)
+        for part in range(2):
+            bring_down(m, part, share)
+
+        @pl.when(m + 1 < micros)
+        def _():
+            send_rows(m + 1)
+
         send_sums(m)
-        for hop in range(3, chips):
-            ahead(functools.partial(relay, m + 1, hop))
+
+        @pl.when(m + 1 < micros)
+        def _():
+            for hop in range(1, chips):
+                relay(m + 1, hop)
+
+        finish(m)
         return carry
 
     lax.fori_loop(0, micros, step_over, 0)
-    finish(micros - 1)
 
     def drain(m, carry):
         for hop in range(chips):

time: 209 us -> 215 us (1.029)
  Pallas kernels: 205 us -> 210 us
    pallas_call x1, Pallas kernels: 205 us -> 210 us  [whole_kernel(): pl.pallas_call(functools.partial(kernel, dims), out_shape=jax.ShapeDtypeS...]
where the time goes in v3:
time: 215 us; the launch traced here: 212 us
  Pallas kernels  210 us (98%)
    pallas_call x1, Pallas kernels, whole_kernel(): pl.pallas_call(functools.partial(kernel, dims), out_shape=jax.ShapeDtypeS...  210 us

profile of v3, /device:TPU:23, one launch (start us, length us, event | category | flops | bytes accessed | tf_op | source)
XLA Modules:
  0.0 211.6 jit_solution(14412726626360115515)
XLA Ops:
  0.0 209.8 %shard_map.64 = bf16[1,6,24,1440]{3,2,1,0:T(8,128)(2,1)} custom-call(bf16[6,24,1440]{2,1,0:T(8,128)(2,1)} %tokens_ref.1, f32[1,1440]{1,0:T(1,128)} %gain_ref.1, bf16[1,1,1440,2880]{3,2,1,0:T(8,128)(2,1)} %gate_up_hbm.1, bf16[1,1,1440,1440]{3,2,1,0:T(8,128)(2,1)} %down_hbm.1, s32[1,6,4,24]{3,2,1,0:T(4,128)} %bitcast.2, s32[1,6,4,24]{3,2,1,0:T(4,128)} %bitcast.3), custom_call_target="tpu_custom_call" | custom-call | flops 14332723200 | bytes 12441600 | tf_op jit(solution)/shard_map/pallas_call | solution.py:457
  209.8 1.8 copy.8

commit v4 on v3

--- a/solution.py
+++ b/solution.py
@@ -100,9 +100,11 @@
 
 def folded(rows, half):
     token_count, width = rows.shape
-    rest = jnp.concatenate(
-        [rows[:, half:], jnp.zeros((token_count, 2 * half - width), rows.dtype)], axis=1
-    )
+    rest = rows[:, half:]
+    if width < 2 * half:
+        rest = jnp.concatenate(
+            [rest, jnp.zeros((token_count, 2 * half - width), rows.dtype)], axis=1
+        )
     return jnp.concatenate([rows[:, :half], rest], axis=0)
 
 
@@ -112,7 +114,7 @@
     out_ref,
     gate_up_w, up_w, down_w, stream, blocks, rows_x, rows_act, partial, sib_out, sib_in,
     sum_out, sum_in, passed, share_lanes,
-    weight_sem, up_send, low_send, lane_recv, fwd_send, sib_send, sib_recv, sum_send, sum_recv,
+    weight_sem, lane_send, lane_recv, fwd_send, sib_send, sib_recv, sum_send, sum_recv,
     pass_send, pass_recv,
 ):
     sections, experts, micros, token_count, width, hidden, half = dims
@@ -165,18 +167,10 @@
 
     gain = folded(gain_ref[...], half)
 
-    def up_copy(m, hop):
-        owner = (chip - hop) * CORES + core
+    def lane_copy(m, step):
         return to(
-            blocks.at[m, owner], blocks.at[m, owner], up_send.at[m, hop],
-            lane_recv.at[m, owner], me + CORES,
-        )
-
-    def low_copy(m, hop):
-        owner = (chip + hop) * CORES + core
-        return to(
-            blocks.at[m, owner], blocks.at[m, owner], low_send.at[m, hop],
-            lane_recv.at[m, owner], me - CORES,
+            blocks.at[m, me], blocks.at[m, me], lane_send.at[m, step], lane_recv.at[m, me],
+            other(step) * CORES + core,
         )
 
     def sibling_copy(m, owner):
@@ -191,11 +185,11 @@
             sib_recv.at[m, part], sibling,
         )
 
-    def sum_copy(m, step):
+    def sum_copy(m, part, step):
         there = other(step)
         return to(
-            sum_out.at[m, there], sum_in.at[m, chip], sum_send.at[m, step],
-            sum_recv.at[m, chip], there * CORES + core,
+            sum_out.at[m, part, there], sum_in.at[m, part, chip], sum_send.at[m, part, step],
+            sum_recv.at[m, part, chip], there * CORES + core,
         )
 
     def pass_copy(m):
@@ -244,41 +238,14 @@
         last = high[:, tile:] + share_lanes[m]
         high = last if tile == 0 else jnp.concatenate([high[:, :tile], last], axis=1)
         blocks[m, me] = jnp.concatenate([low, high], axis=0).astype(BF16)
-        pass_block(m, 0)
-
-    def pass_block(m, hop):
-        @pl.when(jnp.logical_and(chip >= hop, chip + 1 < chips))
-        def _():
-            up_copy(m, hop).start()
-
-        @pl.when(jnp.logical_and(chip + hop < chips, chip > 0))
-        def _():
-            low_copy(m, hop).start()
-
-        if hop == 0:
-            sibling_copy(m, me).start()
-
-    def relay(m, hop):
-        @pl.when(chip >= hop)
-        def _():
-            owner = (chip - hop) * CORES + core
+        for step in range(chips - 1, 0, -1):
+            lane_copy(m, step).start()
+        sibling_copy(m, me).start()
+
+    def forward_rows(m):
+        for step in range(1, chips):
+            owner = other(step) * CORES + core
             got_block(m, owner)
-
-            @pl.when(chip + 1 < chips)
-            def _():
-                up_copy(m, hop).start()
-
-            sibling_copy(m, owner).start()
-
-        @pl.when(chip + hop < chips)
-        def _():
-            owner = (chip + hop) * CORES + core
-            got_block(m, owner)
-
-            @pl.when(chip > 0)
-            def _():
-                low_copy(m, hop).start()
-
             sibling_copy(m, owner).start()
 
     def project(m):
@@ -301,12 +268,14 @@
             rows_act[:, at:upto] = (gate * jax.nn.sigmoid(1.702 * gate) * (up + 1.0)).astype(BF16)
         return share
 
-    def bring_down(m, part, share):
+    def bring_down(m, part, share, between):
         act = rows_act[:, :hidden]
         rows = experts * token_count
         for left in range(0, half, CHUNK):
             at = part * half + left
             room = min(CHUNK, half - left)
+            if left + room == half:
+                between()
             upto = min(at + room, width)
             value = jnp.dot(act, down_w[:, at:upto], preferred_element_type=F32) * share
             if upto - at < room:
@@ -319,28 +288,36 @@
         sib_out[m, part] = partial[1 - core, part].astype(BF16)
         partial_copy(m, part).start()
 
-    def own_sum(there):
+    def own_sum(part, there):
         at = pl.ds(pl.multiple_of(there * token_count, 8), token_count)
-        return jnp.concatenate([partial[core, 0, at, :], partial[core, 1, at, :]], axis=0)
-
-    def send_sums(m):
-        for part in range(2):
-            partial_copy(m, part).wait_recv()
-            partial[core, part] = partial[core, part] + sib_in[m, part].astype(F32)
+        return partial[core, part, at, :]
+
+    def send_sums(m, part):
+        partial_copy(m, part).wait_recv()
+        partial[core, part] = partial[core, part] + sib_in[m, part].astype(F32)
         for step in range(chips - 1, 0, -1):
             there = other(step)
-            sum_out[m, there] = own_sum(there).astype(BF16)
-            sum_copy(m, step).start()
+            sum_out[m, part, there] = folded(own_sum(part, there), half // 2).astype(BF16)
+            sum_copy(m, part, step).start()
 
     def finish(m):
-        total = stream[m].astype(F32) + own_sum(chip)
-        for step in range(1, chips):
-            there = other(step)
-            to(
-                sum_out.at[m, there], sum_in.at[m, there], sum_send.at[m, step],
-                sum_recv.at[m, there], there * CORES + core,
-            ).wait_recv()
-            total = total + sum_in[m, there].astype(F32)
+        total = stream[m].astype(F32)
+        sums = []
+        for part in range(2):
+            quarters = jnp.zeros((2 * token_count, half // 2), F32)
+            for step in range(1, chips):
+                there = other(step)
+                to(
+                    sum_out.at[m, part, there], sum_in.at[m, part, there],
+                    sum_send.at[m, part, step], sum_recv.at[m, part, there],
+                    there * CORES + core,
+                ).wait_recv()
+                quarters = quarters + sum_in[m, part, there].astype(F32)
+            sums.append(
+                own_sum(part, chip)
+                + jnp.concatenate([quarters[:token_count], quarters[token_count:]], axis=1)
+            )
+        total = total + jnp.concatenate(sums, axis=0)
         passed[m] = total.astype(BF16)
 
         @pl.when(section + 1 < sections)
@@ -376,43 +353,35 @@
     def _():
         send_rows(0)
 
-    for hop in range(1, chips):
-        relay(0, hop)
+    forward_rows(0)
 
     def step_over(m, carry):
         share = project(m)
-        for part in range(2):
-            bring_down(m, part, share)
+        bring_down(m, 0, share, lambda: None)
+        bring_down(m, 1, share, lambda: send_sums(m, 0))
+        send_sums(m, 1)
 
         @pl.when(m + 1 < micros)
         def _():
             send_rows(m + 1)
 
-        send_sums(m)
+        finish(m)
 
         @pl.when(m + 1 < micros)
         def _():
-            for hop in range(1, chips):
-                relay(m + 1, hop)
-
-        finish(m)
+            forward_rows(m + 1)
+
         return carry
 
     lax.fori_loop(0, micros, step_over, 0)
 
     def drain(m, carry):
-        for hop in range(chips):
-            @pl.when(jnp.logical_and(chip >= hop, chip + 1 < chips))
-            def _():
-                up_copy(m, hop).wait_send()
-
-            @pl.when(jnp.logical_and(chip + hop < chips, chip > 0))
-            def _():
-                low_copy(m, hop).wait_send()
-
-            sibling_copy(m, hop * CORES + core).wait_send()
+        for step in range(chips):
+            sibling_copy(m, step * CORES + core).wait_send()
         for step in range(1, chips):
-            sum_copy(m, step).wait_send()
+            lane_copy(m, step).wait_send()
+            for part in range(2):
+                sum_copy(m, part, step).wait_send()
         for part in range(2):
             partial_copy(m, part).wait_send()
 
@@ -433,6 +402,8 @@
 def fits_vmem(sections, experts, micros, token_count, width, hidden):
     half = half_width(width)
     chips = experts // CORES
+    if half % (2 * LANES):
+        return False
     block = 2 * token_count * half * 2
     held = micros * block * (experts + 3 * chips + 3) + 2 * experts * block
     held += (2 * hidden + 4 * LANES) * width * 4
@@ -470,19 +441,18 @@
             pltpu.VMEM((CORES, 2, chips * token_count, half), F32),
             pltpu.VMEM((micros, 2, chips * token_count, half), BF16),
             pltpu.VMEM((micros, 2, chips * token_count, half), BF16),
-            pltpu.VMEM((micros, chips, folded_rows, half), BF16),
-            pltpu.VMEM((micros, chips, folded_rows, half), BF16),
+            pltpu.VMEM((micros, 2, chips, folded_rows, half // 2), BF16),
+            pltpu.VMEM((micros, 2, chips, folded_rows, half // 2), BF16),
             pltpu.VMEM((micros, folded_rows, half), BF16),
             pltpu.VMEM((micros, token_count, LANES), F32),
             dma((2,)),
-            dma((micros, chips)),
             dma((micros, chips)),
             dma((micros, experts)),
             dma((micros, chips)),
             dma((micros, 2)),
             dma((micros, 2)),
-            dma((micros, chips)),
-            dma((micros, chips)),
+            dma((micros, 2, chips)),
+            dma((micros, 2, chips)),
             dma((micros,)),
             dma((micros,)),
         ],

time: 215 us -> 201 us (0.935)
  Pallas kernels: 210 us -> 197 us
    pallas_call x1, Pallas kernels: 210 us -> 197 us  [whole_kernel(): pl.pallas_call(functools.partial(kernel, dims), out_shape=jax.ShapeDtypeS...]
where the time goes in v4:
time: 201 us; the launch traced here: 199 us
  Pallas kernels  197 us (98%)
    pallas_call x1, Pallas kernels, whole_kernel(): pl.pallas_call(functools.partial(kernel, dims), out_shape=jax.ShapeDtypeS...  197 us

profile of v4, /device:TPU:23, one launch (start us, length us, event | category | flops | bytes accessed | tf_op | source)
XLA Modules:
  0.0 198.7 jit_solution(7865480363838627171)
XLA Ops:
  0.0 196.8 %shard_map.64 = bf16[1,6,24,1440]{3,2,1,0:T(8,128)(2,1)} custom-call(bf16[6,24,1440]{2,1,0:T(8,128)(2,1)} %tokens_ref.1, f32[1,1440]{1,0:T(1,128)} %gain_ref.1, bf16[1,1,1440,2880]{3,2,1,0:T(8,128)(2,1)} %gate_up_hbm.1, bf16[1,1,1440,1440]{3,2,1,0:T(8,128)(2,1)} %down_hbm.1, s32[1,6,4,24]{3,2,1,0:T(4,128)} %bitcast.2, s32[1,6,4,24]{3,2,1,0:T(4,128)} %bitcast.3), custom_call_target="tpu_custom_call" | custom-call | flops 14332723200 | bytes 12441600 | tf_op jit(solution)/shard_map/pallas_call | solution.py:428
  196.9 1.8 copy.8
